TPU v7x, 512 devices: a whole 4x4x16 slice. The times are simulated.
512 devices in a mesh: dom: 64 (over x, z), sub: 8 (over y, core).
Axes of the slice: x: 4, y: 4, z: 16, core: 2. Of those that a mesh axis runs over, the one named last changes fastest.
Arguments:
- rhs: float32 [204800], P(('dom', 'sub')), may hold values from -6 to 6
- diag_blocks: bfloat16 [2048, 10000], P(('dom', 'sub'))
- face_blocks: bfloat16 [2048, 40000], P(('dom', 'sub')), may hold values from -0.21875 to 0.21875
- precond_blocks: bfloat16 [2048, 10000], P(('dom', 'sub'))
- neighbours: int32 [2048, 4], P(('dom', 'sub')), may hold values from -1 to 2047, as said below
Outputs:
- adjoint: float32 [204800], P(('dom', 'sub'))
Inputs may be any that keep to these rules, and one draw needn't show every extreme that they name: `neighbours`: let element g lie on device d * 8 + s (slab d, position s), g = (d * 8 + s) * 4 + i. Face 1 names an element of device (d + 1, s) or -1; face 0 names one of device (d - 1, s) or -1; faces 2 and 3 name elements of slab d (any position, itself possible). Element e's face 1 names m exactly when m's face 0 names e, and e's face 2 names m exactly when m's face 3 names e. Face 0 is -1 in slab 0, face 1 in the last slab.
All inputs are finite; a program needn't handle non-finite values.
Results may differ from a plain program's by a relative error of at most 0.003.
Values sent between devices are 32-bit elements; how exact they have to be, the bound alone decides.
A program may use at most 64 MiB of HBM per device.

v0:
```python
import jax
import jax.numpy as jnp
from jax import lax
from jax.sharding import PartitionSpec as P

B = 100


def passed_along(value, axis, steps):
    count = lax.axis_size(axis)
    initial, last = (max(0, -steps), min(count, count - steps))
    return lax.ppermute(value, axis, [(source, source + steps) for source in range(initial, last)])


def pick_rows(source, targets, modulus):
    valid = targets >= 0
    index = jnp.where(valid, targets % modulus, 0)
    return jnp.where(valid[:, None], jnp.take(source, index, axis=0), 0.0)


def apply_operator(vector, diag, faces, neighbours):
    elems = neighbours.shape[0]
    subs = lax.axis_size("sub")
    low = vector.reshape(elems, B).astype(jnp.bfloat16)
    image = jnp.einsum("eab,ea->eb", diag, low, preferred_element_type=jnp.float32)
    sent = jnp.einsum("ekab,ea->ekb", faces, low, preferred_element_type=jnp.float32)
    from_below = passed_along(sent[:, 1], "dom", 1)
    from_above = passed_along(sent[:, 0], "dom", -1)
    image = image + pick_rows(from_below, neighbours[:, 0], elems)
    image = image + pick_rows(from_above, neighbours[:, 1], elems)
    second, third = (
        lax.all_gather(sent[:, 2], "sub", axis=0, tiled=True),
        lax.all_gather(sent[:, 3], "sub", axis=0, tiled=True),
    )
    image = image + pick_rows(second, neighbours[:, 3], subs * elems)
    image = image + pick_rows(third, neighbours[:, 2], subs * elems)
    return image.reshape(-1)


def precondition(vector, blocks):
    low = vector.reshape(blocks.shape[0], B).astype(jnp.bfloat16)
    return jnp.einsum("eab,eb->ea", blocks, low, preferred_element_type=jnp.float32).reshape(-1)


def global_sum(value):
    return lax.psum(value, ("dom", "sub"))


def givens_solve(beta, h11, h21, h12, h22, h32):
    first_r = jnp.sqrt(h11 * h11 + h21 * h21)
    cosine = h11 / first_r
    sine = h21 / first_r
    upper = cosine * h12 + sine * h22
    lower = cosine * h22 - sine * h12
    second_r = jnp.sqrt(lower * lower + h32 * h32)
    second_y = lower / second_r * (-sine * beta) / second_r
    first_y = (cosine * beta - upper * second_y) / first_r
    return (first_y, second_y)


def body(rhs, diag_blocks, face_blocks, precond_blocks, neighbours):
    elems = neighbours.shape[0]
    diag = diag_blocks.reshape(elems, B, B)
    faces = face_blocks.reshape(elems, 4, B, B)
    blocks = precond_blocks.reshape(elems, B, B)
    beta = jnp.sqrt(global_sum(jnp.sum(rhs * rhs)))
    basis_one = rhs / beta
    search_one = precondition(basis_one, blocks)
    work = apply_operator(search_one, diag, faces, neighbours)
    h11 = global_sum(jnp.sum(work * basis_one))
    work = work - h11 * basis_one
    h21 = jnp.sqrt(global_sum(jnp.sum(work * work)))
    basis_two = work / h21
    search_two = precondition(basis_two, blocks)
    work = apply_operator(search_two, diag, faces, neighbours)
    h12 = global_sum(jnp.sum(work * basis_one))
    work = work - h12 * basis_one
    h22 = global_sum(jnp.sum(work * basis_two))
    work = work - h22 * basis_two
    h32 = jnp.sqrt(global_sum(jnp.sum(work * work)))
    first_y, second_y = givens_solve(beta, h11, h21, h12, h22, h32)
    return first_y * search_one + second_y * search_two


def solution(mesh):
    placed = (
        P(("dom", "sub")),
        P(("dom", "sub"), None),
        P(("dom", "sub"), None),
        P(("dom", "sub"), None),
        P(("dom", "sub"), None),
    )
    return jax.shard_map(
        body, mesh=mesh, in_specs=placed, out_specs=P(("dom", "sub")), check_vma=False
    )
```

profile of v0, /device:TPU:1, one launch (start us, length us, event | category | flops | bytes accessed | tf_op | source)
XLA Modules:
  0.0 694.6 jit_solution(16542610128314088485)
XLA Ops:
  0.0 1.3 multiply_reduce_fusion.5
  1.3 111.0 %psum.42 = f32[]{:T(128)} all-reduce(f32[]{:T(128)} %multiply_reduce_fusion.5), channel_id=1, replica_groups=mesh['dom'=64,'sub'=8] {'dom','sub'}, use_global_device_ids=true, to_apply=%region_1.0 | all-reduce | flops 1 | bytes 8 | tf_op jit(solution)/shard_map/psum | solution.py:46
  113.0 0.7 fusion.21
  113.8 1.1 reshape.36
  115.0 0.8 reshape.38
  116.1 2.8 collective-permute-start
  118.9 1.3 collective-permute-start.1
  120.6 12.1 %all-gather = f32[32,1,100]{2,1,0:T(1,128)S(1)} all-gather(f32[4,1,100]{2,1,0:T(1,128)S(1)} %bitcast.59), channel_id=2, replica_groups=mesh['dom'=64,'sub'=8] {'sub'}, dimensions={0}, use_global_device_ids=true | all-gather | bytes 14400 | tf_op jit(solution)/shard_map/all_gather | solution.py:32
  133.2 11.3 %all-gather.1 = f32[32,1,100]{2,1,0:T(1,128)S(1)} all-gather(f32[4,1,100]{2,1,0:T(1,128)S(1)} %bitcast.58), channel_id=3, replica_groups=mesh['dom'=64,'sub'=8] {'sub'}, dimensions={0}, use_global_device_ids=true | all-gather | bytes 14400 | tf_op jit(solution)/shard_map/all_gather | solution.py:33
  144.5 0.6 gather_fusion.2
  145.1 0.6 gather_fusion.3
  145.6 0.6 gather_fusion
  146.2 0.6 gather_fusion.1
  146.9 0.6 multiply_reduce_fusion.4
  147.5 101.7 %psum.43 = f32[]{:T(128)} all-reduce(f32[]{:T(128)} %multiply_reduce_fusion.4), channel_id=1, replica_groups=mesh['dom'=64,'sub'=8] {'dom','sub'}, use_global_device_ids=true, to_apply=%region_3.6 | all-reduce | flops 1 | bytes 8 | tf_op jit(solution)/shard_map/psum | solution.py:46
  249.2 1.3 multiply_reduce_fusion.3
  250.6 99.9 %psum.44 = f32[]{:T(128)} all-reduce(f32[]{:T(128)} %multiply_reduce_fusion.3), channel_id=1, replica_groups=mesh['dom'=64,'sub'=8] {'dom','sub'}, use_global_device_ids=true, to_apply=%region_5.8 | all-reduce | flops 1 | bytes 8 | tf_op jit(solution)/shard_map/psum | solution.py:46
  351.2 0.7 fusion.20
  352.5 11.7 %all-gather.2 = f32[32,1,100]{2,1,0:T(1,128)S(1)} all-gather(f32[4,1,100]{2,1,0:T(1,128)S(1)} %bitcast.61), channel_id=4, replica_groups=mesh['dom'=64,'sub'=8] {'sub'}, dimensions={0}, use_global_device_ids=true | all-gather | bytes 14400 | tf_op jit(solution)/shard_map/all_gather | solution.py:32
  364.1 3.0 collective-permute-start.2
  367.2 1.3 collective-permute-start.3
  368.5 11.6 %all-gather.3 = f32[32,1,100]{2,1,0:T(1,128)S(1)} all-gather(f32[4,1,100]{2,1,0:T(1,128)S(1)} %bitcast.60), channel_id=5, replica_groups=mesh['dom'=64,'sub'=8] {'sub'}, dimensions={0}, use_global_device_ids=true | all-gather | bytes 14400 | tf_op jit(solution)/shard_map/all_gather | solution.py:33
  382.1 0.6 gather_fusion.6
  383.2 0.6 gather_fusion.4
  383.8 0.6 gather_fusion.5
  384.5 0.6 multiply_reduce_fusion.2
  385.2 102.5 %psum.45 = f32[]{:T(128)} all-reduce(f32[]{:T(128)} %multiply_reduce_fusion.2), channel_id=1, replica_groups=mesh['dom'=64,'sub'=8] {'dom','sub'}, use_global_device_ids=true, to_apply=%region_7.10 | all-reduce | flops 1 | bytes 8 | tf_op jit(solution)/shard_map/psum | solution.py:46
  487.7 1.2 multiply_reduce_fusion.1
  489.6 100.4 %psum.46 = f32[]{:T(128)} all-reduce(f32[]{:T(128)} %multiply_reduce_fusion.1), channel_id=1, replica_groups=mesh['dom'=64,'sub'=8] {'dom','sub'}, use_global_device_ids=true, to_apply=%region_9.12 | all-reduce | flops 1 | bytes 8 | tf_op jit(solution)/shard_map/psum | solution.py:46
  590.6 1.9 multiply_reduce_fusion
  593.7 99.4 %psum.47 = f32[]{:T(128)} all-reduce(f32[]{:T(128)} %multiply_reduce_fusion), channel_id=1, replica_groups=mesh['dom'=64,'sub'=8] {'dom','sub'}, use_global_device_ids=true, to_apply=%region_11.14 | all-reduce | flops 1 | bytes 8 | tf_op jit(solution)/shard_map/psum | solution.py:46
  694.0 0.7 add.99
  (39 shorter events, 2.7 us)
Async XLA Ops:
  0.0 115.0 %copy-start = (bf16[4,40000]{1,0:T(4,128)(2,1)S(1)}, bf16[4,40000]{1,0:T(4,128)(2,1)}, u32[]{:S(2)}) copy-start(bf16[4,40000]{1,0:T(4,128)(2,1)} %param.11) | copy-start | bytes 960004
  115.9 17.0 %copy-start.2 = (bf16[4,10000]{1,0:T(4,128)(2,1)S(1)}, bf16[4,10000]{1,0:T(4,128)(2,1)}, u32[]{:S(2)}) copy-start(bf16[4,10000]{1,0:T(4,128)(2,1)} %param.10) | copy-start | bytes 240004
  116.1 4.1 copy-start.1
  116.1 29.5 %collective-permute-start = (f32[4,100]{1,0:T(4,128)S(1)}, f32[4,100]{1,0:T(4,128)S(1)}, u32[]{:S(2)}, u32[]{:S(2)}) collective-permute-start(f32[4,100]{1,0:T(4,128)S(1)} %get-tuple-element.31), channel_id=1, source_target_pairs={{0,8},{8,16},{16,24},{24,32},{32,40},{40,48},{48,56},{56,64},{64,7... | collective-permute-start | bytes 4808 | tf_op jit(solution)/shard_map/ppermute | solution.py:12
  118.9 27.3 %collective-permute-start.1 = (f32[4,100]{1,0:T(4,128)S(1)}, f32[4,100]{1,0:T(4,128)S(1)}, u32[]{:S(2)}, u32[]{:S(2)}) collective-permute-start(f32[4,100]{1,0:T(4,128)S(1)} %get-tuple-element.34), channel_id=1, source_target_pairs={{8,0},{16,8},{24,16},{32,24},{40,32},{48,40},{56,48},{64,56},{72,6... | collective-permute-start | bytes 4808 | tf_op jit(solution)/shard_map/ppermute | solution.py:12
  364.1 19.1 %collective-permute-start.2 = (f32[4,100]{1,0:T(4,128)S(1)}, f32[4,100]{1,0:T(4,128)S(1)}, u32[]{:S(2)}, u32[]{:S(2)}) collective-permute-start(f32[4,100]{1,0:T(4,128)S(1)} %get-tuple-element.27), channel_id=1, source_target_pairs={{0,8},{8,16},{16,24},{24,32},{32,40},{40,48},{48,56},{56,64},{64,7... | collective-permute-start | bytes 4808 | tf_op jit(solution)/shard_map/ppermute | solution.py:12
  367.2 16.6 %collective-permute-start.3 = (f32[4,100]{1,0:T(4,128)S(1)}, f32[4,100]{1,0:T(4,128)S(1)}, u32[]{:S(2)}, u32[]{:S(2)}) collective-permute-start(f32[4,100]{1,0:T(4,128)S(1)} %get-tuple-element.30), channel_id=1, source_target_pairs={{8,0},{16,8},{24,16},{32,24},{40,32},{48,40},{56,48},{64,56},{72,6... | collective-permute-start | bytes 4808 | tf_op jit(solution)/shard_map/ppermute | solution.py:12
where the time goes:
time: 696 us; the launch traced here: 695 us
  blocking collectives  662 us (95%)
  other arithmetic  8.8 us (1%)
  starting transfers between devices  8.37 us (1%)
  local copies, waits for them, and re-layouts  7.83 us (1%)
  between operations  6.96 us (1%)
    psum x6, blocking collectives, global_sum(): return lax.psum(value, ('dom', 'sub'))  615 us
    all_gather x2, blocking collectives, apply_operator(): lax.all_gather(sent[:, 2], 'sub', axis=0, tiled=True)  23.8 us
    all_gather x2, blocking collectives, apply_operator(): lax.all_gather(sent[:, 3], 'sub', axis=0, tiled=True)  22.9 us
  transfers between devices with their start and end apart: 4, of which 0 were waited for; matrix products, arithmetic and copies ran while one was open for 1% of the time, Pallas kernels for 0%

commit v1 on v0

v1 whole, which is shorter than its diff:
```python
import functools

import jax
import jax.numpy as jnp
from jax import lax
from jax.experimental import pallas as pl
from jax.experimental.pallas import tpu as pltpu
from jax.sharding import PartitionSpec as P

B = 100
E = 4
LANES = 128
TILES = 25
CHIPS_X = 4
SCALES = (2.0**-44, 1.0, 2.0**44)
SHRINK = 2.0**-12
MESH = pl.DeviceIdType.MESH
F32 = jnp.float32


def lane_of(rows=E):
    return lax.broadcasted_iota(jnp.int32, (rows, LANES), 1)


def periodic(vector):
    lane = lane_of()
    base = jnp.where(lane < B, vector, pltpu.roll(vector, B, 1))
    tiles = []
    for j in range(TILES):
        offset = 28 * j % B
        if offset == 0:
            tiles.append(base)
        else:
            left = pltpu.roll(base, LANES - offset, 1)
            right = pltpu.roll(base, B - offset, 1)
            tiles.append(jnp.where(lane < LANES - offset, left, right))
    return tiles


def tile_at(ref, j):
    width = min(LANES, ref.shape[1] - j * LANES)
    part = ref[:, j * LANES : j * LANES + width].astype(F32)
    if width < LANES:
        part = jnp.concatenate([part, jnp.zeros((E, LANES - width), F32)], axis=1)
    return part


def row_products(ref, vector):
    lane = lane_of()
    tiles = periodic(vector)
    count = -(-B * B // LANES)
    products = [tile_at(ref, j) * tiles[j % TILES] for j in range(count)]
    sums = []
    for a in range(B):
        j, start = divmod(B * a, LANES)
        if start + B <= LANES:
            row = products[j]
            if start > 0:
                row = jnp.where(lane >= start, row, 0.0)
            if start + B < LANES:
                row = jnp.where(lane < start + B, row, 0.0)
        else:
            row = jnp.where(lane >= start, products[j], jnp.where(lane < start + B - LANES, products[j + 1], 0.0))
        sums.append(jnp.sum(row, axis=1, keepdims=True))
    return sums


def fold(tiles):
    lane = lane_of()
    flat = jnp.concatenate(tiles, axis=1)
    width = TILES * LANES
    while width > B:
        width //= 2
        flat = flat[:, :width] + flat[:, width : 2 * width]
    return jnp.concatenate([flat, jnp.zeros((E, LANES - B), F32)], axis=1)


def column_products(ref, first_row, values):
    lane = lane_of()
    start, stop = first_row * B, (first_row + B) * B
    sums = [None] * TILES
    wide = [jnp.broadcast_to(value, (E, LANES)) for value in values]
    for j in range(start // LANES, -(-stop // LANES)):
        factor = None
        for row in range(j * LANES // B, (j * LANES + LANES - 1) // B + 1):
            begin = row * B - j * LANES
            inside = first_row <= row < first_row + B
            value = wide[row - first_row] if inside else jnp.zeros((E, LANES), F32)
            factor = value if factor is None else jnp.where(lane >= begin, value, factor)
        term = tile_at(ref, j) * factor
        slot = j % TILES
        sums[slot] = term if sums[slot] is None else sums[slot] + term
    return fold(sums)


def as_rows(values):
    lane = lane_of()
    out = jnp.zeros((E, LANES), F32)
    for a, value in enumerate(values):
        out = jnp.where(lane == a, value, out)
    return out


def kernel(
    sizes, rhs_hbm, diag_hbm, face_hbm, prec_hbm, near_ref, out_ref,
    rhs_ref, diag_ref, face_ref, prec_ref, load_sem,
    out_box, in_box, plane_box, column_box, plane_out, column_out,
    send_sem, recv_sem, plane_sem, column_sem,
):
    doms, subs = sizes
    chips_z = doms // CHIPS_X
    d, s = lax.axis_index("dom"), lax.axis_index("sub")
    x, z = d // chips_z, d % chips_z
    plane, slab = CHIPS_X * subs, subs * E

    loads = [
        pltpu.make_async_copy(src, dst, load_sem.at[i])
        for i, (src, dst) in enumerate(
            [(rhs_hbm, rhs_ref), (prec_hbm, prec_ref), (diag_hbm, diag_ref), (face_hbm, face_ref)]
        )
    ]
    for load in loads:
        load.start()

    def plane_mate(k):
        return ((x + k // subs) % CHIPS_X) * chips_z + z, (s + k % subs) % subs

    def column_mate(k):
        return x * chips_z + (z + k) % chips_z, s

    above, below = (d + 1) % doms, (d + doms - 1) % doms
    barrier = pltpu.get_barrier_semaphore()

    def greet(device):
        pl.semaphore_signal(barrier, inc=1, device_id=device, device_id_type=MESH)

    greet((above, s))
    greet((below, s))

    @pl.loop(1, plane)
    def _(k):
        greet(plane_mate(k))

    @pl.loop(1, chips_z)
    def _(k):
        greet(column_mate(k))

    goal = {}
    for e in range(E):
        for face in range(4):
            near = near_ref[e, face]
            if face >= 2:
                row = (near - d * slab - s * E + slab) % slab
            else:
                row = near % E + slab + (E if face == 0 else 0)
            goal[e, face] = jnp.where(near >= 0, row, -1)

    def apply(vector, step):
        if step == 0:
            loads[1].wait()
        values = row_products(prec_ref, vector)
        if step == 0:
            loads[3].wait()
        sent = [column_products(face_ref, face * B, values) for face in range(4)]
        row = lax.broadcasted_iota(jnp.int32, (slab, LANES), 0)
        inner = jnp.zeros((slab, LANES), F32)
        for face in (2, 3):
            for e in range(E):
                inner = inner + jnp.where(row == goal[e, face], sent[face][e : e + 1], 0.0)
        row = lax.broadcasted_iota(jnp.int32, (2 * E, LANES), 0) + slab
        outer = jnp.zeros((2 * E, LANES), F32)
        for face in (0, 1):
            for e in range(E):
                outer = outer + jnp.where(row == goal[e, face], sent[face][e : e + 1], 0.0)
        for k in range(1, subs):
            out_box[step, k - 1] = inner[E * k : E * k + E]
        out_box[step, subs - 1] = outer[:E]
        out_box[step, subs] = outer[E:]
        if step == 0:
            pl.semaphore_wait(barrier, plane - 1 + chips_z - 1 + 2)
        for k in range(subs + 1):
            if k < subs - 1:
                device = (d, (s + k + 1) % subs)
            else:
                device = (above if k == subs - 1 else below, s)
            pltpu.make_async_remote_copy(
                src_ref=out_box.at[step, k],
                dst_ref=in_box.at[step, k],
                send_sem=send_sem.at[step],
                recv_sem=recv_sem.at[step],
                device_id=device,
                device_id_type=MESH,
            ).start()
        if step == 0:
            loads[2].wait()
        image = inner[:E] + column_products(diag_ref, 0, values)
        search = as_rows(values)
        pltpu.make_async_copy(in_box.at[step], in_box.at[step], recv_sem.at[step]).wait()
        for k in range(subs + 1):
            image = image + in_box[step, k]
        return search, image

    loads[0].wait()
    flat = jnp.concatenate([rhs_ref[...] * SHRINK, jnp.zeros((1, E * LANES - E * B), F32)], axis=1)
    start = jnp.concatenate([flat[:, B * e : B * e + B] for e in range(E)], axis=0)
    start = jnp.concatenate([start, jnp.zeros((E, LANES - B), F32)], axis=1)
    search_one, image_one = apply(start, 0)
    search_two, image_two = apply(image_one, 1)

    products = [image_one * start, image_two * start]
    for scale in SCALES:
        one, two = image_one * scale, image_two * (scale * scale)
        products += [one * one, one * two, two * two]
    lane = lane_of(1)
    message = jnp.zeros((1, LANES), F32)
    for q, product in enumerate(products):
        total = jnp.sum(jnp.sum(product, axis=0, keepdims=True), axis=1, keepdims=True)
        message = jnp.where(lane == q, total, message)

    def share(message, mate, count, box, out, sems):
        out[...] = message

        @pl.loop(1, count)
        def _(k):
            pltpu.make_async_remote_copy(
                src_ref=out,
                dst_ref=box.at[pl.ds(k, 1)],
                send_sem=sems.at[0],
                recv_sem=sems.at[1],
                device_id=mate(k),
                device_id_type=MESH,
            ).start()

        box[0:1] = message
        arrived = box.at[pl.ds(1, count - 1)]
        pltpu.make_async_copy(arrived, arrived, sems.at[1]).wait()
        return jnp.sum(box[...], axis=0, keepdims=True)

    message = share(message, plane_mate, plane, plane_box, plane_out, plane_sem)
    message = share(message, column_mate, chips_z, column_box, column_out, column_sem)

    def entry(q):
        return jnp.sum(jnp.where(lane == q, message, 0.0), axis=1, keepdims=True)

    def pick(q):
        low, mid, high = (entry(2 + 3 * i + q) for i in range(3))
        return jnp.where(too_large, low, jnp.where(too_small, high, mid))

    size = entry(2 + 3 + 2)
    too_large = jnp.logical_not(size < 1e26)
    too_small = size < 1e-26
    scale = jnp.where(too_large, SCALES[0], jnp.where(too_small, SCALES[2], SCALES[1]))
    one_one, one_two, two_two = pick(0), pick(1), pick(2)
    one_rhs, two_rhs = entry(0) * scale, entry(1) * scale * scale
    slope = one_two / one_one
    rest = jnp.maximum(two_two - slope * one_two, two_two * 2.0**-22)
    second = (two_rhs - slope * one_rhs) / rest
    first = one_rhs / one_one - slope * second
    answer = first * scale * (search_one * (1.0 / SHRINK)) + second * scale * scale * (search_two * (1.0 / SHRINK))
    out_ref[...] = jnp.concatenate([answer[e : e + 1, :B] for e in range(E)], axis=1)

    for step in range(2):
        pltpu.make_async_copy(out_box.at[step], out_box.at[step], send_sem.at[step]).wait()
    for box, count, sems in ((plane_box, plane, plane_sem), (column_box, chips_z, column_sem)):
        sent = box.at[pl.ds(1, count - 1)]
        pltpu.make_async_copy(sent, sent, sems.at[0]).wait()


def solution(mesh):
    doms, subs = mesh.shape["dom"], mesh.shape["sub"]
    chips_z = doms // CHIPS_X

    def body(rhs, diag, faces, precond, neighbours):
        out = pl.pallas_call(
            functools.partial(kernel, (doms, subs)),
            out_shape=jax.ShapeDtypeStruct((1, E * B), F32),
            in_specs=[pl.BlockSpec(memory_space=pltpu.HBM)] * 4 + [pl.BlockSpec(memory_space=pltpu.SMEM)],
            out_specs=pl.BlockSpec(memory_space=pltpu.VMEM),
            scratch_shapes=[
                pltpu.VMEM((1, E * B), F32),
                pltpu.VMEM(diag.shape, diag.dtype),
                pltpu.VMEM(faces.shape, faces.dtype),
                pltpu.VMEM(precond.shape, precond.dtype),
                pltpu.SemaphoreType.DMA((4,)),
                pltpu.VMEM((2, subs + 1, E, LANES), F32),
                pltpu.VMEM((2, subs + 1, E, LANES), F32),
                pltpu.VMEM((CHIPS_X * subs, LANES), F32),
                pltpu.VMEM((chips_z, LANES), F32),
                pltpu.VMEM((1, LANES), F32),
                pltpu.VMEM((1, LANES), F32),
                pltpu.SemaphoreType.DMA((2,)),
                pltpu.SemaphoreType.DMA((2,)),
                pltpu.SemaphoreType.DMA((2,)),
                pltpu.SemaphoreType.DMA((2,)),
            ],
            compiler_params=pltpu.CompilerParams(
                collective_id=0, has_side_effects=True, vmem_limit_bytes=32 * 2**20
            ),
            cost_estimate=pl.CostEstimate(flops=2_000_000, bytes_accessed=500_000, transcendentals=0),
        )(rhs.reshape(1, -1), diag, faces, precond, neighbours)
        return out.reshape(-1)

    rows = P(("dom", "sub"), None)
    flat = P(("dom", "sub"))
    return jax.shard_map(
        body, mesh=mesh, in_specs=(flat, rows, rows, rows, rows), out_specs=flat, check_vma=False
    )
```

time: 696 us -> 42.4 us (0.06)
  blocking collectives: 662 us -> 0 us
  Pallas kernels: 0 us -> 37.4 us
  other arithmetic: 8.8 us -> 0 us
  starting transfers between devices: 8.37 us -> 0 us
    psum x6 -> x0, blocking collectives: 615 us -> none  [global_sum(): return lax.psum(value, ('dom', 'sub'))]
    all_gather x4 -> x0, blocking collectives: 46.7 us -> none  [the longest x2 23.8 us: apply_operator(): lax.all_gather(sent[:, 2], 'sub', axis=0, tiled=True)]
    pallas_call x0 -> x1, Pallas kernels: none -> 37.4 us  [body(): pl.pallas_call(functools.partial(kernel, (doms, subs)), out_shape=jax.Sha...]
    ppermute x4 -> x0, starting transfers between devices: 8.37 us -> none  [passed_along(): lax.ppermute(value, axis, [(source, source + steps) for source in range(i...]
    reduce_sum x6 -> x0, other arithmetic: 7 us -> none  [the longest x1 1.89 us: body(): h32 = jnp.sqrt(global_sum(jnp.sum(work * work)))]
  transfers between devices with their start and end apart: 4 -> 0, of which waited for: 0 -> 0; matrix products, arithmetic and copies ran while one was open for 1% -> 0% of each run, Pallas kernels for 0% -> 0%
where the time goes in v1:
time: 42.4 us; the launch traced here: 42.1 us
  Pallas kernels  37.4 us (88%)
  local copies, waits for them, and re-layouts  4.69 us (11%)
    pallas_call x1, Pallas kernels, body(): pl.pallas_call(functools.partial(kernel, (doms, subs)), out_shape=jax.Sha...  37.4 us
    unnamed x11, local copies, waits for them, and re-layouts  4.69 us

profile of v1, /device:TPU:1, one launch (start us, length us, event | category | flops | bytes accessed | tf_op | source)
XLA Modules:
  0.0 42.1 jit_solution(2752916286101744433)
XLA Ops:
  0.0 0.0 copy-start
  0.0 1.0 %copy-done = bf16[4,40000]{1,0:T(4,128)(2,1)S(1)} copy-done((bf16[4,40000]{1,0:T(4,128)(2,1)S(1)}, bf16[4,40000]{1,0:T(4,128)(2,1)}, u32[]{:S(2)}) %copy-start) | copy-done | bytes 320024
  1.0 0.0 copy-start.1
  1.0 0.9 %copy-done.1 = bf16[4,10000]{1,0:T(4,128)(2,1)S(1)} copy-done((bf16[4,10000]{1,0:T(4,128)(2,1)S(1)}, bf16[4,10000]{1,0:T(4,128)(2,1)}, u32[]{:S(2)}) %copy-start.1) | copy-done | bytes 80024
  1.9 0.0 copy-start.2
  1.9 0.9 %copy-done.2 = bf16[4,10000]{1,0:T(4,128)(2,1)S(1)} copy-done((bf16[4,10000]{1,0:T(4,128)(2,1)S(1)}, bf16[4,10000]{1,0:T(4,128)(2,1)}, u32[]{:S(2)}) %copy-start.2) | copy-done | bytes 80024
  2.7 0.0 copy-start.3
  2.7 0.7 %copy-done.3 = f32[400]{0:T(512)S(1)} copy-done((f32[400]{0:T(512)S(1)}, f32[400]{0:T(512)}, u32[]{:S(2)}) %copy-start.3) | copy-done | bytes 1624
  3.4 0.0 copy-start.4
  3.4 0.7 %copy-done.4 = s32[4,4]{1,0:T(4,128)S(1)} copy-done((s32[4,4]{1,0:T(4,128)S(1)}, s32[4,4]{1,0:T(4,128)}, u32[]{:S(2)}) %copy-start.4) | copy-done | bytes 88
  4.1 37.4 %shard_map.55 = f32[1,400]{1,0:T(1,128)S(1)} custom-call(f32[1,400]{1,0:T(1,128)S(1)} %bitcast.3, bf16[4,10000]{1,0:T(4,128)(2,1)S(1)} %copy-done.1, bf16[4,40000]{1,0:T(4,128)(2,1)S(1)} %copy-done, bf16[4,10000]{1,0:T(4,128)(2,1)S(1)} %copy-done.2, s32[4,4]{1,0:T(4,128)S(1)} %copy-done.4), custom_call_target="tpu_custom_call" | custom-call | flops 2000000 | bytes 500000 | tf_op jit(solution)/shard_map/pallas_call | solution.py:274
  41.5 0.6 %copy.7 = f32[400]{0:T(512)} copy(f32[400]{0:T(512)S(1)} %bitcast.2) | data formatting | bytes 3200
Async XLA Ops:
  0.0 1.0 %copy-start = (bf16[4,40000]{1,0:T(4,128)(2,1)S(1)}, bf16[4,40000]{1,0:T(4,128)(2,1)}, u32[]{:S(2)}) copy-start(bf16[4,40000]{1,0:T(4,128)(2,1)} %face_hbm.1) | copy-start | bytes 960004
  1.0 0.9 %copy-start.1 = (bf16[4,10000]{1,0:T(4,128)(2,1)S(1)}, bf16[4,10000]{1,0:T(4,128)(2,1)}, u32[]{:S(2)}) copy-start(bf16[4,10000]{1,0:T(4,128)(2,1)} %diag_hbm.1) | copy-start | bytes 240004
  1.9 0.9 %copy-start.2 = (bf16[4,10000]{1,0:T(4,128)(2,1)S(1)}, bf16[4,10000]{1,0:T(4,128)(2,1)}, u32[]{:S(2)}) copy-start(bf16[4,10000]{1,0:T(4,128)(2,1)} %prec_hbm.1) | copy-start | bytes 240004
  2.7 0.7 %copy-start.3 = (f32[400]{0:T(512)S(1)}, f32[400]{0:T(512)}, u32[]{:S(2)}) copy-start(f32[400]{0:T(512)} %param.5) | copy-start | bytes 4804
  3.4 0.7 %copy-start.4 = (s32[4,4]{1,0:T(4,128)S(1)}, s32[4,4]{1,0:T(4,128)}, u32[]{:S(2)}) copy-start(s32[4,4]{1,0:T(4,128)} %near_ref.1) | copy-start | bytes 196

commit v2 on v1

--- a/solution.py
+++ b/solution.py
@@ -102,10 +102,10 @@
 
 
 def kernel(
-    sizes, rhs_hbm, diag_hbm, face_hbm, prec_hbm, near_ref, out_ref,
-    rhs_ref, diag_ref, face_ref, prec_ref, load_sem,
+    sizes, rhs_hbm, diag_hbm, face_hbm, prec_hbm, near_hbm, out_ref,
+    rhs_ref, diag_ref, face_ref, prec_ref, near_ref, load_sem,
     out_box, in_box, plane_box, column_box, plane_out, column_out,
-    send_sem, recv_sem, plane_sem, column_sem,
+    send_sem, recv_sem, plane_sem, column_sem, known_a, known_b, known_c,
 ):
     doms, subs = sizes
     chips_z = doms // CHIPS_X
@@ -116,7 +116,10 @@
     loads = [
         pltpu.make_async_copy(src, dst, load_sem.at[i])
         for i, (src, dst) in enumerate(
-            [(rhs_hbm, rhs_ref), (prec_hbm, prec_ref), (diag_hbm, diag_ref), (face_hbm, face_ref)]
+            [
+                (rhs_hbm, rhs_ref), (prec_hbm, prec_ref), (face_hbm, face_ref), (near_hbm, near_ref),
+                (diag_hbm, diag_ref),
+            ]
         )
     ]
     for load in loads:
@@ -131,36 +134,45 @@
     above, below = (d + 1) % doms, (d + doms - 1) % doms
     barrier = pltpu.get_barrier_semaphore()
 
-    def greet(device):
-        pl.semaphore_signal(barrier, inc=1, device_id=device, device_id_type=MESH)
-
-    greet((above, s))
-    greet((below, s))
-
-    @pl.loop(1, plane)
-    def _(k):
-        greet(plane_mate(k))
-
-    @pl.loop(1, chips_z)
-    def _(k):
-        greet(column_mate(k))
-
-    goal = {}
-    for e in range(E):
-        for face in range(4):
-            near = near_ref[e, face]
-            if face >= 2:
-                row = (near - d * slab - s * E + slab) % slab
-            else:
-                row = near % E + slab + (E if face == 0 else 0)
-            goal[e, face] = jnp.where(near >= 0, row, -1)
+    def tell(semaphore, device):
+        pl.semaphore_signal(semaphore, inc=1, device_id=device, device_id_type=MESH)
+
+    def along_z(step):
+        return x * chips_z + (z + step + chips_z) % chips_z, s
+
+    def along_x(step):
+        return (x + step + CHIPS_X) % CHIPS_X * chips_z + z, s
+
+    def greet():
+        for k in range(1, subs):
+            tell(barrier, (d, (s + k) % subs))
+        for device in ((above, s), (below, s), along_z(1), along_z(-1), along_x(1), along_x(-1)):
+            tell(barrier, device)
+
+    greeted = subs - 1 + 6
+
+    def tell_a():
+        for device in (along_z(1), along_z(-1), along_x(1), along_x(-1)):
+            tell(known_a, device)
+
+    def tell_b():
+        pl.semaphore_wait(known_a, 4)
+        for device in (along_z(2), along_z(-2), along_x(1)):
+            tell(known_b, device)
+
+    def tell_c():
+        pl.semaphore_wait(known_b, 3)
+        for device in (along_z(4), along_z(-4)):
+            tell(known_c, device)
+
+    greet()
 
     def apply(vector, step):
         if step == 0:
             loads[1].wait()
         values = row_products(prec_ref, vector)
         if step == 0:
-            loads[3].wait()
+            loads[2].wait()
         sent = [column_products(face_ref, face * B, values) for face in range(4)]
         row = lax.broadcasted_iota(jnp.int32, (slab, LANES), 0)
         inner = jnp.zeros((slab, LANES), F32)
@@ -177,7 +189,7 @@
         out_box[step, subs - 1] = outer[:E]
         out_box[step, subs] = outer[E:]
         if step == 0:
-            pl.semaphore_wait(barrier, plane - 1 + chips_z - 1 + 2)
+            pl.semaphore_wait(barrier, greeted)
         for k in range(subs + 1):
             if k < subs - 1:
                 device = (d, (s + k + 1) % subs)
@@ -192,13 +204,26 @@
                 device_id_type=MESH,
             ).start()
         if step == 0:
-            loads[2].wait()
+            tell_a()
+            loads[4].wait()
         image = inner[:E] + column_products(diag_ref, 0, values)
         search = as_rows(values)
+        tell_b() if step == 0 else tell_c()
         pltpu.make_async_copy(in_box.at[step], in_box.at[step], recv_sem.at[step]).wait()
         for k in range(subs + 1):
             image = image + in_box[step, k]
         return search, image
+
+    loads[3].wait()
+    goal = {}
+    for e in range(E):
+        for face in range(4):
+            near = near_ref[e, face]
+            if face >= 2:
+                row = (near - d * slab - s * E + slab) % slab
+            else:
+                row = near % E + slab + (E if face == 0 else 0)
+            goal[e, face] = jnp.where(near >= 0, row, -1)
 
     loads[0].wait()
     flat = jnp.concatenate([rhs_ref[...] * SHRINK, jnp.zeros((1, E * LANES - E * B), F32)], axis=1)
@@ -237,6 +262,7 @@
         return jnp.sum(box[...], axis=0, keepdims=True)
 
     message = share(message, plane_mate, plane, plane_box, plane_out, plane_sem)
+    pl.semaphore_wait(known_c, 2)
     message = share(message, column_mate, chips_z, column_box, column_out, column_sem)
 
     def entry(q):
@@ -273,15 +299,16 @@
     def body(rhs, diag, faces, precond, neighbours):
         out = pl.pallas_call(
             functools.partial(kernel, (doms, subs)),
-            out_shape=jax.ShapeDtypeStruct((1, E * B), F32),
-            in_specs=[pl.BlockSpec(memory_space=pltpu.HBM)] * 4 + [pl.BlockSpec(memory_space=pltpu.SMEM)],
+            out_shape=pltpu.VMEM((1, E * B), F32),
+            in_specs=[pl.BlockSpec(memory_space=pltpu.HBM)] * 5,
             out_specs=pl.BlockSpec(memory_space=pltpu.VMEM),
             scratch_shapes=[
                 pltpu.VMEM((1, E * B), F32),
                 pltpu.VMEM(diag.shape, diag.dtype),
                 pltpu.VMEM(faces.shape, faces.dtype),
                 pltpu.VMEM(precond.shape, precond.dtype),
-                pltpu.SemaphoreType.DMA((4,)),
+                pltpu.SMEM(neighbours.shape, neighbours.dtype),
+                pltpu.SemaphoreType.DMA((5,)),
                 pltpu.VMEM((2, subs + 1, E, LANES), F32),
                 pltpu.VMEM((2, subs + 1, E, LANES), F32),
                 pltpu.VMEM((CHIPS_X * subs, LANES), F32),
@@ -292,9 +319,12 @@
                 pltpu.SemaphoreType.DMA((2,)),
                 pltpu.SemaphoreType.DMA((2,)),
                 pltpu.SemaphoreType.DMA((2,)),
+                pltpu.SemaphoreType.REGULAR,
+                pltpu.SemaphoreType.REGULAR,
+                pltpu.SemaphoreType.REGULAR,
             ],
             compiler_params=pltpu.CompilerParams(
-                collective_id=0, has_side_effects=True, vmem_limit_bytes=32 * 2**20
+                collective_id=0, has_side_effects=True, vmem_limit_bytes=62 * 2**20
             ),
             cost_estimate=pl.CostEstimate(flops=2_000_000, bytes_accessed=500_000, transcendentals=0),
         )(rhs.reshape(1, -1), diag, faces, precond, neighbours)

time: 42.4 us -> 34 us (0.80)
  local copies, waits for them, and re-layouts: 4.69 us -> 0.58 us
  Pallas kernels: 37.4 us -> 33.3 us
    pallas_call x1, Pallas kernels: 37.4 us -> 33.3 us  [body(): pl.pallas_call(functools.partial(kernel, (doms, subs)), out_shape=pltpu.V...]
    unnamed x11 -> x1, local copies, waits for them, and re-layouts: 4.69 us -> 0.58 us
where the time goes in v2:
time: 34 us; the launch traced here: 33.8 us
  Pallas kernels  33.3 us (98%)
  local copies, waits for them, and re-layouts  0.58 us (2%)
    pallas_call x1, Pallas kernels, body(): pl.pallas_call(functools.partial(kernel, (doms, subs)), out_shape=pltpu.V...  33.3 us

profile of v2, /device:TPU:1, one launch (start us, length us, event | category | flops | bytes accessed | tf_op | source)
XLA Modules:
  0.0 33.8 jit_solution(7276179821571014058)
XLA Ops:
  0.0 33.3 %shard_map.55 = f32[1,400]{1,0:T(1,128)S(1)} custom-call(f32[1,400]{1,0:T(1,128)} %bitcast.3, bf16[4,10000]{1,0:T(4,128)(2,1)} %diag_hbm.1, bf16[4,40000]{1,0:T(4,128)(2,1)} %face_hbm.1, bf16[4,10000]{1,0:T(4,128)(2,1)} %prec_hbm.1, s32[4,4]{1,0:T(4,128)} %near_hbm.1), custom_call_target="tpu_custom_call" | custom-call | flops 2000000 | bytes 500000 | tf_op jit(solution)/shard_map/pallas_call | solution.py:300
  33.3 0.6 %copy.7 = f32[400]{0:T(512)} copy(f32[400]{0:T(512)S(1)} %bitcast.2) | data formatting | bytes 3200

commit v3 on v2

v3 whole, which is shorter than its diff:
```python
import functools

import jax
import jax.numpy as jnp
from jax import lax
from jax.experimental import pallas as pl
from jax.experimental.pallas import tpu as pltpu
from jax.sharding import PartitionSpec as P

B = 100
E = 4
LANES = 128
TILES = 25
CHIPS_X = 4
SCALES = (2.0**-44, 1.0, 2.0**44)
SHRINK = 2.0**-12
MESH = pl.DeviceIdType.MESH
F32 = jnp.float32


def lane_of(rows=E):
    return lax.broadcasted_iota(jnp.int32, (rows, LANES), 1)


def periodic(vector):
    lane = lane_of()
    base = jnp.where(lane < B, vector, pltpu.roll(vector, B, 1))
    tiles = []
    for j in range(TILES):
        offset = 28 * j % B
        if offset == 0:
            tiles.append(base)
        else:
            left = pltpu.roll(base, LANES - offset, 1)
            right = pltpu.roll(base, B - offset, 1)
            tiles.append(jnp.where(lane < LANES - offset, left, right))
    return tiles


def tile_at(ref, j):
    width = min(LANES, ref.shape[1] - j * LANES)
    part = ref[:, j * LANES : j * LANES + width].astype(F32)
    if width < LANES:
        part = jnp.concatenate([part, jnp.zeros((E, LANES - width), F32)], axis=1)
    return part


def row_products(ref, vector):
    lane = lane_of()
    tiles = periodic(vector)
    count = -(-B * B // LANES)
    products = [tile_at(ref, j) * tiles[j % TILES] for j in range(count)]
    sums = []
    for a in range(B):
        j, start = divmod(B * a, LANES)
        if start + B <= LANES:
            row = products[j]
            if start > 0:
                row = jnp.where(lane >= start, row, 0.0)
            if start + B < LANES:
                row = jnp.where(lane < start + B, row, 0.0)
        else:
            row = jnp.where(lane >= start, products[j], jnp.where(lane < start + B - LANES, products[j + 1], 0.0))
        sums.append(jnp.sum(row, axis=1, keepdims=True))
    return sums


def fold(tiles):
    lane = lane_of()
    flat = jnp.concatenate(tiles, axis=1)
    width = TILES * LANES
    while width > B:
        width //= 2
        flat = flat[:, :width] + flat[:, width : 2 * width]
    return jnp.concatenate([flat, jnp.zeros((E, LANES - B), F32)], axis=1)


def column_products(ref, first_row, values):
    lane = lane_of()
    start, stop = first_row * B, (first_row + B) * B
    sums = [None] * TILES
    wide = [jnp.broadcast_to(value, (E, LANES)) for value in values]
    for j in range(start // LANES, -(-stop // LANES)):
        factor = None
        for row in range(j * LANES // B, (j * LANES + LANES - 1) // B + 1):
            begin = row * B - j * LANES
            inside = first_row <= row < first_row + B
            value = wide[row - first_row] if inside else jnp.zeros((E, LANES), F32)
            factor = value if factor is None else jnp.where(lane >= begin, value, factor)
        term = tile_at(ref, j) * factor
        slot = j % TILES
        sums[slot] = term if sums[slot] is None else sums[slot] + term
    return fold(sums)


def as_rows(values):
    lane = lane_of()
    out = jnp.zeros((E, LANES), F32)
    for a, value in enumerate(values):
        out = jnp.where(lane == a, value, out)
    return out


def kernel(
    sizes, rhs_hbm, diag_hbm, face_hbm, prec_hbm, near_hbm, out_ref,
    rhs_ref, diag_ref, face_ref, prec_ref, near_ref, load_sem,
    inner_out, outer_out, inner_one, outer_one, inner_two, outer_two, rhs_box, own_box, own_out, sum_box, sum_out,
    sems, known_a, known_b, known_c, known_d,
):
    doms, subs = sizes
    chips_z = doms // CHIPS_X
    d, s = lax.axis_index("dom"), lax.axis_index("sub")
    x, z = d // chips_z, d % chips_z
    slab = subs * E

    loads = [
        pltpu.make_async_copy(src, dst, load_sem.at[i])
        for i, (src, dst) in enumerate(
            [
                (rhs_hbm, rhs_ref), (prec_hbm, prec_ref), (face_hbm, face_ref), (near_hbm, near_ref),
                (diag_hbm, diag_ref),
            ]
        )
    ]
    for load in loads:
        load.start()

    mates = [(s + k) % subs for k in range(subs)]
    rows_x = [(x + k) % CHIPS_X * chips_z for k in range(CHIPS_X)]
    rows_z = [(z + k) % chips_z for k in range(chips_z)]
    far_first = sorted(range(1, subs), key=lambda k: -min(k // 2, subs // 2 - k // 2))
    above, below = (d + 1) % doms, (d + doms - 1) % doms

    def along_z(step):
        return rows_x[0] + rows_z[step % chips_z], s

    def along_x(step):
        return rows_x[step % CHIPS_X] + z, s

    barrier = pltpu.get_barrier_semaphore()

    def tell(semaphore, devices):
        for device in devices:
            pl.semaphore_signal(semaphore, inc=1, device_id=device, device_id_type=MESH)

    beside = [(above, s), (below, s), along_z(1), along_z(-1), along_x(1), along_x(-1)]
    tell(barrier, [(d, mates[k]) for k in far_first] + beside)

    def tell_a():
        tell(known_a, beside)

    def tell_b():
        pl.semaphore_wait(known_a, len(beside))
        tell(known_b, [along_z(2), along_z(-2), along_z(1), along_z(-1)])

    def tell_c():
        pl.semaphore_wait(known_b, 4)
        tell(known_c, [along_z(4), along_z(-4)])

    def tell_d():
        pl.semaphore_wait(known_c, 2)
        tell(known_d, [along_z(2), along_z(-2)])

    def send(src, dst, device, group):
        pltpu.make_async_remote_copy(
            src_ref=src,
            dst_ref=dst,
            send_sem=sems.at[group, 0],
            recv_sem=sems.at[group, 1],
            device_id=device,
            device_id_type=MESH,
        ).start()

    filled = [
        inner_one, outer_one, inner_two, outer_two, rhs_box.at[pl.ds(0, subs - 1)], own_box.at[pl.ds(0, subs - 1)],
        sum_box.at[pl.ds(1, doms - 1)],
    ]
    INNER_ONE, OUTER_ONE, INNER_TWO, OUTER_TWO, RHS, OWN, SUM = range(7)

    def arrived(*groups):
        for group in groups:
            pltpu.make_async_copy(filled[group], filled[group], sems.at[group, 1]).wait()

    loads[3].wait()
    goal = {}
    for e in range(E):
        for face in range(4):
            near = near_ref[e, face]
            row = near - d * slab if face >= 2 else near % E + (E if face == 0 else 0)
            goal[e, face] = jnp.where(near >= 0, row, -1)

    def placed(rows, faces, sent):
        row = lax.broadcasted_iota(jnp.int32, (rows, LANES), 0)
        out = jnp.zeros((rows, LANES), F32)
        for face in faces:
            for e in range(E):
                out = out + jnp.where(row == goal[e, face], sent[face][e : e + 1], 0.0)
        return out

    def outer_of(values):
        sent = {face: column_products(face_ref, face * B, values) for face in (0, 1)}
        return placed(2 * E, (0, 1), sent)

    def inner_of(values):
        sent = {face: column_products(face_ref, face * B, values) for face in (2, 3)}
        return placed(slab, (2, 3), sent)

    def store_slab(ref, value):
        for k in range(subs):
            ref[k] = value[E * k : E * k + E]

    loads[0].wait()
    flat = jnp.concatenate([rhs_ref[...] * SHRINK, jnp.zeros((1, E * LANES - E * B), F32)], axis=1)
    start = jnp.concatenate([flat[:, B * e : B * e + B] for e in range(E)], axis=0)
    start = jnp.concatenate([start, jnp.zeros((E, LANES - B), F32)], axis=1)
    rhs_box[s] = start

    loads[1].wait()
    values = row_products(prec_ref, start)
    loads[2].wait()
    store_slab(inner_out.at[0], inner_of(values))
    outer = outer_of(values)
    outer_out[0, 0] = outer[:E]
    outer_out[0, 1] = outer[E:]
    pl.semaphore_wait(barrier, subs - 1 + len(beside))
    for k in far_first:
        send(inner_out.at[0, mates[k]], inner_one.at[k - 1], (d, mates[k]), INNER_ONE)
    send(outer_out.at[0, 0], outer_one.at[0], (above, s), OUTER_ONE)
    send(outer_out.at[0, 1], outer_one.at[1], (below, s), OUTER_ONE)
    tell_a()
    for k in far_first:
        send(rhs_box.at[s], rhs_box.at[s], (d, mates[k]), RHS)
    loads[4].wait()
    image = inner_out[0, s] + column_products(diag_ref, 0, values)
    search_one = as_rows(values)
    tell_b()
    tell_c()
    arrived(INNER_ONE, OUTER_ONE)
    for k in range(subs - 1):
        image = image + inner_one[k]
    image = image + outer_one[0] + outer_one[1]

    values = row_products(prec_ref, image)
    outer = outer_of(values)
    outer_out[1, 0] = outer[:E]
    outer_out[1, 1] = outer[E:]
    for k in far_first + [0]:
        send(outer_out.at[1, 0], outer_two.at[0, s], (above, mates[k]), OUTER_TWO)
        send(outer_out.at[1, 1], outer_two.at[1, s], (below, mates[k]), OUTER_TWO)
    store_slab(inner_out.at[1], inner_of(values))
    for k in far_first:
        send(inner_out.at[1], inner_two.at[k - 1], (d, mates[k]), INNER_TWO)
    own_out[0] = image
    own_out[1] = column_products(diag_ref, 0, values)
    for k in far_first:
        send(own_out, own_box.at[s], (d, mates[k]), OWN)
    own_box[s] = own_out[...]
    search_two = as_rows(values)
    tell_d()
    arrived(RHS, OUTER_TWO, INNER_TWO, OWN)

    products = []
    for k in range(subs):
        rhs, one = rhs_box[k], own_box[k, 0]
        two = own_box[k, 1] + outer_two[0, k] + outer_two[1, k] + inner_out[1, k]
        for m in range(subs - 1):
            two = two + inner_two[m, k]
        terms = [one * rhs, two * rhs]
        for scale in SCALES:
            low_one, low_two = one * scale, two * (scale * scale)
            terms += [low_one * low_one, low_one * low_two, low_two * low_two]
        products = [a + b for a, b in zip(products, terms)] if products else terms
    lane = lane_of(1)
    row = lax.broadcasted_iota(jnp.int32, (16, LANES), 0)
    table = jnp.zeros((16, LANES), F32)
    for q, product in enumerate(products):
        table = jnp.where(row == q, jnp.sum(product, axis=0, keepdims=True), table)
    table = jnp.where(row == lane_of(16), jnp.sum(table, axis=1, keepdims=True), 0.0)
    message = jnp.sum(table, axis=0, keepdims=True)

    pl.semaphore_wait(known_d, 2)
    sum_out[...] = message
    sum_box[0:1] = message
    for k_z in sorted(range(chips_z), key=lambda k: -min(k, chips_z - k)):
        for k_x in sorted(range(CHIPS_X), key=lambda k: -min(k, CHIPS_X - k)):
            k = k_x * chips_z + k_z
            if k:
                send(sum_out, sum_box.at[pl.ds(k, 1)], (rows_x[k_x] + rows_z[k_z], s), SUM)
    arrived(SUM)
    message = jnp.sum(sum_box[...], axis=0, keepdims=True)

    def entry(q):
        return jnp.sum(jnp.where(lane == q, message, 0.0), axis=1, keepdims=True)

    def pick(q):
        low, mid, high = (entry(2 + 3 * i + q) for i in range(3))
        return jnp.where(too_large, low, jnp.where(too_small, high, mid))

    size = entry(2 + 3 + 2)
    too_large = jnp.logical_not(size < 1e26)
    too_small = size < 1e-26
    scale = jnp.where(too_large, SCALES[0], jnp.where(too_small, SCALES[2], SCALES[1]))
    one_one, one_two, two_two = pick(0), pick(1), pick(2)
    one_rhs, two_rhs = entry(0) * scale, entry(1) * scale * scale
    slope = one_two / one_one
    rest = jnp.maximum(two_two - slope * one_two, two_two * 2.0**-22)
    second = (two_rhs - slope * one_rhs) / rest
    first = one_rhs / one_one - slope * second
    answer = first * scale * (search_one * (1.0 / SHRINK)) + second * scale * scale * (search_two * (1.0 / SHRINK))
    out_ref[...] = jnp.concatenate([answer[e : e + 1, :B] for e in range(E)], axis=1)

    for group, ref in enumerate(filled):
        pltpu.make_async_copy(ref, ref, sems.at[group, 0]).wait()


def solution(mesh):
    doms, subs = mesh.shape["dom"], mesh.shape["sub"]

    def body(rhs, diag, faces, precond, neighbours):
        out = pl.pallas_call(
            functools.partial(kernel, (doms, subs)),
            out_shape=pltpu.VMEM((1, E * B), F32),
            in_specs=[pl.BlockSpec(memory_space=pltpu.HBM)] * 5,
            out_specs=pl.BlockSpec(memory_space=pltpu.VMEM),
            scratch_shapes=[
                pltpu.VMEM((1, E * B), F32),
                pltpu.VMEM(diag.shape, diag.dtype),
                pltpu.VMEM(faces.shape, faces.dtype),
                pltpu.VMEM(precond.shape, precond.dtype),
                pltpu.SMEM(neighbours.shape, neighbours.dtype),
                pltpu.SemaphoreType.DMA((5,)),
                pltpu.VMEM((2, subs, E, LANES), F32),
                pltpu.VMEM((2, 2, E, LANES), F32),
                pltpu.VMEM((subs - 1, E, LANES), F32),
                pltpu.VMEM((2, E, LANES), F32),
                pltpu.VMEM((subs - 1, subs, E, LANES), F32),
                pltpu.VMEM((2, subs, E, LANES), F32),
                pltpu.VMEM((subs, E, LANES), F32),
                pltpu.VMEM((subs, 2, E, LANES), F32),
                pltpu.VMEM((2, E, LANES), F32),
                pltpu.VMEM((doms, LANES), F32),
                pltpu.VMEM((1, LANES), F32),
                pltpu.SemaphoreType.DMA((7, 2)),
                pltpu.SemaphoreType.REGULAR,
                pltpu.SemaphoreType.REGULAR,
                pltpu.SemaphoreType.REGULAR,
                pltpu.SemaphoreType.REGULAR,
            ],
            compiler_params=pltpu.CompilerParams(
                collective_id=0, has_side_effects=True, vmem_limit_bytes=62 * 2**20
            ),
            cost_estimate=pl.CostEstimate(flops=2_000_000, bytes_accessed=500_000, transcendentals=0),
        )(rhs.reshape(1, -1), diag, faces, precond, neighbours)
        return out.reshape(-1)

    rows = P(("dom", "sub"), None)
    flat = P(("dom", "sub"))
    return jax.shard_map(
        body, mesh=mesh, in_specs=(flat, rows, rows, rows, rows), out_specs=flat, check_vma=False
    )
```

time: 34 us -> 32.4 us (0.953)
  Pallas kernels: 33.3 us -> 31.7 us
    pallas_call x1, Pallas kernels: 33.3 us -> 31.7 us  [body(): pl.pallas_call(functools.partial(kernel, (doms, subs)), out_shape=pltpu.V...]
where the time goes in v3:
time: 32.4 us; the launch traced here: 32.3 us
  Pallas kernels  31.7 us (98%)
  local copies, waits for them, and re-layouts  0.58 us (2%)
    pallas_call x1, Pallas kernels, body(): pl.pallas_call(functools.partial(kernel, (doms, subs)), out_shape=pltpu.V...  31.7 us

profile of v3, /device:TPU:1, one launch (start us, length us, event | category | flops | bytes accessed | tf_op | source)
XLA Modules:
  0.0 32.3 jit_solution(10335024250530820916)
XLA Ops:
  0.0 31.7 %shard_map.55 = f32[1,400]{1,0:T(1,128)S(1)} custom-call(f32[1,400]{1,0:T(1,128)} %bitcast.3, bf16[4,10000]{1,0:T(4,128)(2,1)} %diag_hbm.1, bf16[4,40000]{1,0:T(4,128)(2,1)} %face_hbm.1, bf16[4,10000]{1,0:T(4,128)(2,1)} %prec_hbm.1, s32[4,4]{1,0:T(4,128)} %near_hbm.1), custom_call_target="tpu_custom_call" | custom-call | flops 2000000 | bytes 500000 | tf_op jit(solution)/shard_map/pallas_call | solution.py:320
  31.7 0.6 %copy.7 = f32[400]{0:T(512)} copy(f32[400]{0:T(512)S(1)} %bitcast.2) | data formatting | bytes 3200

commit v4 on v3

--- a/solution.py
+++ b/solution.py
@@ -93,17 +93,33 @@
     return fold(sums)
 
 
+def unfold(ref, row):
+    j, start = divmod(row * B, LANES)
+    part = tile_at(ref, j)
+    if start + B > LANES:
+        part = jnp.where(lane_of() >= start, part, tile_at(ref, j + 1))
+    return pltpu.roll(part, LANES - start, 1) if start else part
+
+
+def weighted(ref, values, rows):
+    sums = [None] * 4
+    for a, value in enumerate(values):
+        term = ref[a] * value[:rows]
+        sums[a % 4] = term if sums[a % 4] is None else sums[a % 4] + term
+    return jnp.where(lane_of(rows) < B, (sums[0] + sums[1]) + (sums[2] + sums[3]), 0.0)
+
+
 def as_rows(values):
     lane = lane_of()
     out = jnp.zeros((E, LANES), F32)
     for a, value in enumerate(values):
-        out = jnp.where(lane == a, value, out)
+        out = jnp.where(lane == a, value[:E], out)
     return out
 
 
 def kernel(
     sizes, rhs_hbm, diag_hbm, face_hbm, prec_hbm, near_hbm, out_ref,
-    rhs_ref, diag_ref, face_ref, prec_ref, near_ref, load_sem,
+    rhs_ref, diag_ref, face_ref, prec_ref, near_ref, prec_rows, diag_rows, outer_rows, inner_rows, load_sem,
     inner_out, outer_out, inner_one, outer_one, inner_two, outer_two, rhs_box, own_box, own_out, sum_box, sum_out,
     sems, known_a, known_b, known_c, known_d,
 ):
@@ -122,9 +138,6 @@
             ]
         )
     ]
-    for load in loads:
-        load.start()
-
     mates = [(s + k) % subs for k in range(subs)]
     rows_x = [(x + k) % CHIPS_X * chips_z for k in range(CHIPS_X)]
     rows_z = [(z + k) % chips_z for k in range(chips_z)]
@@ -144,7 +157,10 @@
             pl.semaphore_signal(semaphore, inc=1, device_id=device, device_id_type=MESH)
 
     beside = [(above, s), (below, s), along_z(1), along_z(-1), along_x(1), along_x(-1)]
-    tell(barrier, [(d, mates[k]) for k in far_first] + beside)
+    tell(barrier, [(d, mates[k]) for k in far_first])
+    for load in loads:
+        load.start()
+    tell(barrier, beside)
 
     def tell_a():
         tell(known_a, beside)
@@ -192,18 +208,13 @@
     def placed(rows, faces, sent):
         row = lax.broadcasted_iota(jnp.int32, (rows, LANES), 0)
         out = jnp.zeros((rows, LANES), F32)
-        for face in faces:
+        for i, face in enumerate(faces):
             for e in range(E):
-                out = out + jnp.where(row == goal[e, face], sent[face][e : e + 1], 0.0)
+                out = out + jnp.where(row == goal[e, face], sent[E * i + e : E * i + e + 1], 0.0)
         return out
 
-    def outer_of(values):
-        sent = {face: column_products(face_ref, face * B, values) for face in (0, 1)}
-        return placed(2 * E, (0, 1), sent)
-
-    def inner_of(values):
-        sent = {face: column_products(face_ref, face * B, values) for face in (2, 3)}
-        return placed(slab, (2, 3), sent)
+    def pair_products(faces, values):
+        return jnp.concatenate([column_products(face_ref, face * B, values) for face in faces], axis=0)
 
     def store_slab(ref, value):
         for k in range(subs):
@@ -218,13 +229,13 @@
     loads[1].wait()
     values = row_products(prec_ref, start)
     loads[2].wait()
-    store_slab(inner_out.at[0], inner_of(values))
-    outer = outer_of(values)
-    outer_out[0, 0] = outer[:E]
-    outer_out[0, 1] = outer[E:]
+    store_slab(inner_out.at[0], placed(slab, (2, 3), pair_products((2, 3), values)))
     pl.semaphore_wait(barrier, subs - 1 + len(beside))
     for k in far_first:
         send(inner_out.at[0, mates[k]], inner_one.at[k - 1], (d, mates[k]), INNER_ONE)
+    outer = placed(2 * E, (0, 1), pair_products((0, 1), values))
+    outer_out[0, 0] = outer[:E]
+    outer_out[0, 1] = outer[E:]
     send(outer_out.at[0, 0], outer_one.at[0], (above, s), OUTER_ONE)
     send(outer_out.at[0, 1], outer_one.at[1], (below, s), OUTER_ONE)
     tell_a()
@@ -233,6 +244,13 @@
     loads[4].wait()
     image = inner_out[0, s] + column_products(diag_ref, 0, values)
     search_one = as_rows(values)
+
+    for a in range(B):
+        row = unfold(prec_ref, a)
+        prec_rows[a] = jnp.concatenate([row, row], axis=0)
+        diag_rows[a] = unfold(diag_ref, a)
+        outer_rows[a] = jnp.concatenate([unfold(face_ref, a), unfold(face_ref, B + a)], axis=0)
+        inner_rows[a] = jnp.concatenate([unfold(face_ref, 2 * B + a), unfold(face_ref, 3 * B + a)], axis=0)
     tell_b()
     tell_c()
     arrived(INNER_ONE, OUTER_ONE)
@@ -240,18 +258,19 @@
         image = image + inner_one[k]
     image = image + outer_one[0] + outer_one[1]
 
-    values = row_products(prec_ref, image)
-    outer = outer_of(values)
+    twice = jnp.concatenate([image, image], axis=0)
+    values = [jnp.sum(prec_rows[a] * twice, axis=1, keepdims=True) for a in range(B)]
+    outer = placed(2 * E, (0, 1), weighted(outer_rows, values, 2 * E))
     outer_out[1, 0] = outer[:E]
     outer_out[1, 1] = outer[E:]
     for k in far_first + [0]:
         send(outer_out.at[1, 0], outer_two.at[0, s], (above, mates[k]), OUTER_TWO)
         send(outer_out.at[1, 1], outer_two.at[1, s], (below, mates[k]), OUTER_TWO)
-    store_slab(inner_out.at[1], inner_of(values))
+    store_slab(inner_out.at[1], placed(slab, (2, 3), weighted(inner_rows, values, 2 * E)))
     for k in far_first:
         send(inner_out.at[1], inner_two.at[k - 1], (d, mates[k]), INNER_TWO)
     own_out[0] = image
-    own_out[1] = column_products(diag_ref, 0, values)
+    own_out[1] = weighted(diag_rows, values, E)
     for k in far_first:
         send(own_out, own_box.at[s], (d, mates[k]), OWN)
     own_box[s] = own_out[...]
@@ -328,6 +347,10 @@
                 pltpu.VMEM(faces.shape, faces.dtype),
                 pltpu.VMEM(precond.shape, precond.dtype),
                 pltpu.SMEM(neighbours.shape, neighbours.dtype),
+                pltpu.VMEM((B, 2 * E, LANES), F32),
+                pltpu.VMEM((B, E, LANES), F32),
+                pltpu.VMEM((B, 2 * E, LANES), F32),
+                pltpu.VMEM((B, 2 * E, LANES), F32),
                 pltpu.SemaphoreType.DMA((5,)),
                 pltpu.VMEM((2, subs, E, LANES), F32),
                 pltpu.VMEM((2, 2, E, LANES), F32),

time: 32.4 us -> 31.7 us (0.978)
  Pallas kernels: 31.7 us -> 31 us
    pallas_call x1, Pallas kernels: 31.7 us -> 31 us  [body(): pl.pallas_call(functools.partial(kernel, (doms, subs)), out_shape=pltpu.V...]
where the time goes in v4:
time: 31.7 us; the launch traced here: 31.6 us
  Pallas kernels  31 us (98%)
  local copies, waits for them, and re-layouts  0.58 us (2%)
    pallas_call x1, Pallas kernels, body(): pl.pallas_call(functools.partial(kernel, (doms, subs)), out_shape=pltpu.V...  31 us

profile of v4, /device:TPU:1, one launch (start us, length us, event | category | flops | bytes accessed | tf_op | source)
XLA Modules:
  0.0 31.6 jit_solution(8573228925619782439)
XLA Ops:
  0.0 31.0 %shard_map.55 = f32[1,400]{1,0:T(1,128)S(1)} custom-call(f32[1,400]{1,0:T(1,128)} %bitcast.3, bf16[4,10000]{1,0:T(4,128)(2,1)} %diag_hbm.1, bf16[4,40000]{1,0:T(4,128)(2,1)} %face_hbm.1, bf16[4,10000]{1,0:T(4,128)(2,1)} %prec_hbm.1, s32[4,4]{1,0:T(4,128)} %near_hbm.1), custom_call_target="tpu_custom_call" | custom-call | flops 2000000 | bytes 500000 | tf_op jit(solution)/shard_map/pallas_call | solution.py:339
  31.0 0.6 %copy.7 = f32[400]{0:T(512)} copy(f32[400]{0:T(512)S(1)} %bitcast.2) | data formatting | bytes 3200

commit v5 on v4

--- a/solution.py
+++ b/solution.py
@@ -25,15 +25,13 @@
 def periodic(vector):
     lane = lane_of()
     base = jnp.where(lane < B, vector, pltpu.roll(vector, B, 1))
+    rolled = {LANES: base}
+    for shift in range(4, LANES, 4):
+        rolled[shift] = pltpu.roll(base, shift, 1)
     tiles = []
     for j in range(TILES):
         offset = 28 * j % B
-        if offset == 0:
-            tiles.append(base)
-        else:
-            left = pltpu.roll(base, LANES - offset, 1)
-            right = pltpu.roll(base, B - offset, 1)
-            tiles.append(jnp.where(lane < LANES - offset, left, right))
+        tiles.append(jnp.where(lane < LANES - offset, rolled[LANES - offset], rolled[B - offset]))
     return tiles
 
 
@@ -67,12 +65,16 @@
 
 def fold(tiles):
     lane = lane_of()
-    flat = jnp.concatenate(tiles, axis=1)
-    width = TILES * LANES
-    while width > B:
-        width //= 2
-        flat = flat[:, :width] + flat[:, width : 2 * width]
-    return jnp.concatenate([flat, jnp.zeros((E, LANES - B), F32)], axis=1)
+    sums = [None] * 4
+    for row in range(TILES * LANES // B):
+        j, start = divmod(row * B, LANES)
+        part = tiles[j]
+        if start + B > LANES:
+            part = jnp.where(lane >= start, part, tiles[j + 1])
+        if start:
+            part = pltpu.roll(part, LANES - start, 1)
+        sums[row % 4] = part if sums[row % 4] is None else sums[row % 4] + part
+    return jnp.where(lane < B, (sums[0] + sums[1]) + (sums[2] + sums[3]), 0.0)
 
 
 def column_products(ref, first_row, values):
@@ -129,12 +131,14 @@
     x, z = d // chips_z, d % chips_z
     slab = subs * E
 
+    split = 2 * B * B // LANES * LANES
+    early, late = pl.ds(0, split), pl.ds(split, 4 * B * B - split)
     loads = [
         pltpu.make_async_copy(src, dst, load_sem.at[i])
         for i, (src, dst) in enumerate(
             [
-                (rhs_hbm, rhs_ref), (prec_hbm, prec_ref), (face_hbm, face_ref), (near_hbm, near_ref),
-                (diag_hbm, diag_ref),
+                (rhs_hbm, rhs_ref), (prec_hbm, prec_ref), (face_hbm.at[:, late], face_ref.at[:, late]), (near_hbm, near_ref),
+                (diag_hbm, diag_ref), (face_hbm.at[:, early], face_ref.at[:, early]),
             ]
         )
     ]
@@ -197,13 +201,7 @@
         for group in groups:
             pltpu.make_async_copy(filled[group], filled[group], sems.at[group, 1]).wait()
 
-    loads[3].wait()
     goal = {}
-    for e in range(E):
-        for face in range(4):
-            near = near_ref[e, face]
-            row = near - d * slab if face >= 2 else near % E + (E if face == 0 else 0)
-            goal[e, face] = jnp.where(near >= 0, row, -1)
 
     def placed(rows, faces, sent):
         row = lax.broadcasted_iota(jnp.int32, (rows, LANES), 0)
@@ -229,10 +227,17 @@
     loads[1].wait()
     values = row_products(prec_ref, start)
     loads[2].wait()
+    loads[3].wait()
+    for e in range(E):
+        for face in range(4):
+            near = near_ref[e, face]
+            row = near - d * slab if face >= 2 else near % E + (E if face == 0 else 0)
+            goal[e, face] = jnp.where(near >= 0, row, -1)
     store_slab(inner_out.at[0], placed(slab, (2, 3), pair_products((2, 3), values)))
     pl.semaphore_wait(barrier, subs - 1 + len(beside))
     for k in far_first:
         send(inner_out.at[0, mates[k]], inner_one.at[k - 1], (d, mates[k]), INNER_ONE)
+    loads[5].wait()
     outer = placed(2 * E, (0, 1), pair_products((0, 1), values))
     outer_out[0, 0] = outer[:E]
     outer_out[0, 1] = outer[E:]
@@ -275,6 +280,10 @@
         send(own_out, own_box.at[s], (d, mates[k]), OWN)
     own_box[s] = own_out[...]
     search_two = as_rows(values)
+    flat_one, flat_two = (
+        jnp.concatenate([rows[e : e + 1, :B] * (1.0 / SHRINK) for e in range(E)], axis=1)
+        for rows in (search_one, search_two)
+    )
     tell_d()
     arrived(RHS, OUTER_TWO, INNER_TWO, OWN)
 
@@ -325,8 +334,7 @@
     rest = jnp.maximum(two_two - slope * one_two, two_two * 2.0**-22)
     second = (two_rhs - slope * one_rhs) / rest
     first = one_rhs / one_one - slope * second
-    answer = first * scale * (search_one * (1.0 / SHRINK)) + second * scale * scale * (search_two * (1.0 / SHRINK))
-    out_ref[...] = jnp.concatenate([answer[e : e + 1, :B] for e in range(E)], axis=1)
+    out_ref[...] = first * scale * flat_one + second * scale * scale * flat_two
 
     for group, ref in enumerate(filled):
         pltpu.make_async_copy(ref, ref, sems.at[group, 0]).wait()
@@ -351,7 +359,7 @@
                 pltpu.VMEM((B, E, LANES), F32),
                 pltpu.VMEM((B, 2 * E, LANES), F32),
                 pltpu.VMEM((B, 2 * E, LANES), F32),
-                pltpu.SemaphoreType.DMA((5,)),
+                pltpu.SemaphoreType.DMA((6,)),
                 pltpu.VMEM((2, subs, E, LANES), F32),
                 pltpu.VMEM((2, 2, E, LANES), F32),
                 pltpu.VMEM((subs - 1, E, LANES), F32),

time: 31.7 us -> 31.6 us (level)
  no operation moved by 1% of the time
where the time goes in v5:
time: 31.6 us; the launch traced here: 31.4 us
  Pallas kernels  30.8 us (97%)
  local copies, waits for them, and re-layouts  0.58 us (2%)
    pallas_call x1, Pallas kernels, body(): pl.pallas_call(functools.partial(kernel, (doms, subs)), out_shape=pltpu.V...  30.8 us

profile of v5, /device:TPU:1, one launch (start us, length us, event | category | flops | bytes accessed | tf_op | source)
XLA Modules:
  0.0 31.4 jit_solution(7703483701200019591)
XLA Ops:
  0.0 30.8 %shard_map.55 = f32[1,400]{1,0:T(1,128)S(1)} custom-call(f32[1,400]{1,0:T(1,128)} %bitcast.3, bf16[4,10000]{1,0:T(4,128)(2,1)} %diag_hbm.1, bf16[4,40000]{1,0:T(4,128)(2,1)} %face_hbm.1, bf16[4,10000]{1,0:T(4,128)(2,1)} %prec_hbm.1, s32[4,4]{1,0:T(4,128)} %near_hbm.1), custom_call_target="tpu_custom_call" | custom-call | flops 2000000 | bytes 500000 | tf_op jit(solution)/shard_map/pallas_call | solution.py:347
  30.9 0.6 %copy.7 = f32[400]{0:T(512)} copy(f32[400]{0:T(512)S(1)} %bitcast.2) | data formatting | bytes 3200

commit v6 on v5

--- a/solution.py
+++ b/solution.py
@@ -131,14 +131,12 @@
     x, z = d // chips_z, d % chips_z
     slab = subs * E
 
-    split = 2 * B * B // LANES * LANES
-    early, late = pl.ds(0, split), pl.ds(split, 4 * B * B - split)
     loads = [
         pltpu.make_async_copy(src, dst, load_sem.at[i])
         for i, (src, dst) in enumerate(
             [
-                (rhs_hbm, rhs_ref), (prec_hbm, prec_ref), (face_hbm.at[:, late], face_ref.at[:, late]), (near_hbm, near_ref),
-                (diag_hbm, diag_ref), (face_hbm.at[:, early], face_ref.at[:, early]),
+                (rhs_hbm, rhs_ref), (prec_hbm, prec_ref), (face_hbm, face_ref), (near_hbm, near_ref),
+                (diag_hbm, diag_ref),
             ]
         )
     ]
@@ -237,7 +235,6 @@
     pl.semaphore_wait(barrier, subs - 1 + len(beside))
     for k in far_first:
         send(inner_out.at[0, mates[k]], inner_one.at[k - 1], (d, mates[k]), INNER_ONE)
-    loads[5].wait()
     outer = placed(2 * E, (0, 1), pair_products((0, 1), values))
     outer_out[0, 0] = outer[:E]
     outer_out[0, 1] = outer[E:]
@@ -359,7 +356,7 @@
                 pltpu.VMEM((B, E, LANES), F32),
                 pltpu.VMEM((B, 2 * E, LANES), F32),
                 pltpu.VMEM((B, 2 * E, LANES), F32),
-                pltpu.SemaphoreType.DMA((6,)),
+                pltpu.SemaphoreType.DMA((5,)),
                 pltpu.VMEM((2, subs, E, LANES), F32),
                 pltpu.VMEM((2, 2, E, LANES), F32),
                 pltpu.VMEM((subs - 1, E, LANES), F32),

time: 31.6 us -> 31.6 us (level)
  no operation moved by 1% of the time
where the time goes in v6:
time: 31.6 us; the launch traced here: 31.5 us
  Pallas kernels  30.9 us (98%)
  local copies, waits for them, and re-layouts  0.58 us (2%)
    pallas_call x1, Pallas kernels, body(): pl.pallas_call(functools.partial(kernel, (doms, subs)), out_shape=pltpu.V...  30.9 us

profile of v6, /device:TPU:1, one launch (start us, length us, event | category | flops | bytes accessed | tf_op | source)
XLA Modules:
  0.0 31.5 jit_solution(4913298387283844008)
XLA Ops:
  0.0 30.9 %shard_map.55 = f32[1,400]{1,0:T(1,128)S(1)} custom-call(f32[1,400]{1,0:T(1,128)} %bitcast.3, bf16[4,10000]{1,0:T(4,128)(2,1)} %diag_hbm.1, bf16[4,40000]{1,0:T(4,128)(2,1)} %face_hbm.1, bf16[4,10000]{1,0:T(4,128)(2,1)} %prec_hbm.1, s32[4,4]{1,0:T(4,128)} %near_hbm.1), custom_call_target="tpu_custom_call" | custom-call | flops 2000000 | bytes 500000 | tf_op jit(solution)/shard_map/pallas_call | solution.py:344
  30.9 0.6 %copy.7 = f32[400]{0:T(512)} copy(f32[400]{0:T(512)S(1)} %bitcast.2) | data formatting | bytes 3200

commit v7 on v5

--- a/solution.py
+++ b/solution.py
@@ -122,7 +122,7 @@
 def kernel(
     sizes, rhs_hbm, diag_hbm, face_hbm, prec_hbm, near_hbm, out_ref,
     rhs_ref, diag_ref, face_ref, prec_ref, near_ref, prec_rows, diag_rows, outer_rows, inner_rows, load_sem,
-    inner_out, outer_out, inner_one, outer_one, inner_two, outer_two, rhs_box, own_box, own_out, sum_box, sum_out,
+    inner_out, outer_out, inner_one, outer_one, inner_two, outer_two, rhs_box, own_box, sum_box, sum_out,
     sems, known_a, known_b, known_c, known_d,
 ):
     doms, subs = sizes
@@ -271,33 +271,45 @@
     for k in far_first + [0]:
         send(outer_out.at[1, 0], outer_two.at[0, s], (above, mates[k]), OUTER_TWO)
         send(outer_out.at[1, 1], outer_two.at[1, s], (below, mates[k]), OUTER_TWO)
+    own_box[s] = image
+    for k in far_first:
+        send(own_box.at[s], own_box.at[s], (d, mates[k]), OWN)
+    own = weighted(diag_rows, values, E)
     store_slab(inner_out.at[1], placed(slab, (2, 3), weighted(inner_rows, values, 2 * E)))
+    inner_out[1, s] = inner_out[1, s] + own
     for k in far_first:
         send(inner_out.at[1], inner_two.at[k - 1], (d, mates[k]), INNER_TWO)
-    own_out[0] = image
-    own_out[1] = weighted(diag_rows, values, E)
-    for k in far_first:
-        send(own_out, own_box.at[s], (d, mates[k]), OWN)
-    own_box[s] = own_out[...]
     search_two = as_rows(values)
     flat_one, flat_two = (
         jnp.concatenate([rows[e : e + 1, :B] * (1.0 / SHRINK) for e in range(E)], axis=1)
         for rows in (search_one, search_two)
     )
     tell_d()
-    arrived(RHS, OUTER_TWO, INNER_TWO, OWN)
-
-    products = []
-    for k in range(subs):
-        rhs, one = rhs_box[k], own_box[k, 0]
-        two = own_box[k, 1] + outer_two[0, k] + outer_two[1, k] + inner_out[1, k]
+
+    def over_slab(terms):
+        return functools.reduce(lambda a, b: [p + q for p, q in zip(a, b)], [terms(k) for k in range(subs)])
+
+    def early_terms(k):
+        one = own_box[k]
+        return [one * rhs_box[k]] + [(one * scale) * (one * scale) for scale in SCALES]
+
+    def late_terms(k):
+        two = (outer_two[0, k] + outer_two[1, k]) + inner_out[1, k]
         for m in range(subs - 1):
             two = two + inner_two[m, k]
-        terms = [one * rhs, two * rhs]
+        terms = [two * rhs_box[k]]
         for scale in SCALES:
-            low_one, low_two = one * scale, two * (scale * scale)
-            terms += [low_one * low_one, low_one * low_two, low_two * low_two]
-        products = [a + b for a, b in zip(products, terms)] if products else terms
+            low_one, low_two = own_box[k] * scale, two * (scale * scale)
+            terms += [low_one * low_two, low_two * low_two]
+        return terms
+
+    arrived(RHS, OWN)
+    early = over_slab(early_terms)
+    arrived(OUTER_TWO, INNER_TWO)
+    late = over_slab(late_terms)
+    products = [early[0], late[0]]
+    for i in range(len(SCALES)):
+        products += [early[1 + i], late[1 + 2 * i], late[2 + 2 * i]]
     lane = lane_of(1)
     row = lax.broadcasted_iota(jnp.int32, (16, LANES), 0)
     table = jnp.zeros((16, LANES), F32)
@@ -367,8 +379,7 @@
                 pltpu.VMEM((subs - 1, subs, E, LANES), F32),
                 pltpu.VMEM((2, subs, E, LANES), F32),
                 pltpu.VMEM((subs, E, LANES), F32),
-                pltpu.VMEM((subs, 2, E, LANES), F32),
-                pltpu.VMEM((2, E, LANES), F32),
+                pltpu.VMEM((subs, E, LANES), F32),
                 pltpu.VMEM((doms, LANES), F32),
                 pltpu.VMEM((1, LANES), F32),
                 pltpu.SemaphoreType.DMA((7, 2)),

time: 31.6 us -> 31.4 us (level)
  no operation moved by 1% of the time
where the time goes in v7:
time: 31.4 us; the launch traced here: 31.3 us
  Pallas kernels  30.7 us (98%)
  local copies, waits for them, and re-layouts  0.58 us (2%)
    pallas_call x1, Pallas kernels, body(): pl.pallas_call(functools.partial(kernel, (doms, subs)), out_shape=pltpu.V...  30.7 us

profile of v7, /device:TPU:1, one launch (start us, length us, event | category | flops | bytes accessed | tf_op | source)
XLA Modules:
  0.0 31.3 jit_solution(12670585811716009361)
XLA Ops:
  0.0 30.7 %shard_map.55 = f32[1,400]{1,0:T(1,128)S(1)} custom-call(f32[1,400]{1,0:T(1,128)} %bitcast.3, bf16[4,10000]{1,0:T(4,128)(2,1)} %diag_hbm.1, bf16[4,40000]{1,0:T(4,128)(2,1)} %face_hbm.1, bf16[4,10000]{1,0:T(4,128)(2,1)} %prec_hbm.1, s32[4,4]{1,0:T(4,128)} %near_hbm.1), custom_call_target="tpu_custom_call" | custom-call | flops 2000000 | bytes 500000 | tf_op jit(solution)/shard_map/pallas_call | solution.py:359
  30.7 0.6 %copy.7 = f32[400]{0:T(512)} copy(f32[400]{0:T(512)S(1)} %bitcast.2) | data formatting | bytes 3200

commit v8 on v7

--- a/solution.py
+++ b/solution.py
@@ -268,17 +268,22 @@
     outer = placed(2 * E, (0, 1), weighted(outer_rows, values, 2 * E))
     outer_out[1, 0] = outer[:E]
     outer_out[1, 1] = outer[E:]
-    for k in far_first + [0]:
-        send(outer_out.at[1, 0], outer_two.at[0, s], (above, mates[k]), OUTER_TWO)
-        send(outer_out.at[1, 1], outer_two.at[1, s], (below, mates[k]), OUTER_TWO)
+
+    def send_outer(places):
+        for k in places:
+            send(outer_out.at[1, 0], outer_two.at[0, s], (above, mates[k]), OUTER_TWO)
+            send(outer_out.at[1, 1], outer_two.at[1, s], (below, mates[k]), OUTER_TWO)
+
+    send_outer(far_first[:2])
     own_box[s] = image
-    for k in far_first:
-        send(own_box.at[s], own_box.at[s], (d, mates[k]), OWN)
     own = weighted(diag_rows, values, E)
     store_slab(inner_out.at[1], placed(slab, (2, 3), weighted(inner_rows, values, 2 * E)))
     inner_out[1, s] = inner_out[1, s] + own
     for k in far_first:
         send(inner_out.at[1], inner_two.at[k - 1], (d, mates[k]), INNER_TWO)
+    send_outer(far_first[2:] + [0])
+    for k in far_first:
+        send(own_box.at[s], own_box.at[s], (d, mates[k]), OWN)
     search_two = as_rows(values)
     flat_one, flat_two = (
         jnp.concatenate([rows[e : e + 1, :B] * (1.0 / SHRINK) for e in range(E)], axis=1)

time: 31.4 us -> 31.4 us (level)
  no operation moved by 1% of the time
where the time goes in v8:
time: 31.4 us; the launch traced here: 31.3 us
  Pallas kernels  30.7 us (98%)
  local copies, waits for them, and re-layouts  0.58 us (2%)
    pallas_call x1, Pallas kernels, body(): pl.pallas_call(functools.partial(kernel, (doms, subs)), out_shape=pltpu.V...  30.7 us

profile of v8, /device:TPU:1, one launch (start us, length us, event | category | flops | bytes accessed | tf_op | source)
XLA Modules:
  0.0 31.3 jit_solution(11409609228704336045)
XLA Ops:
  0.0 30.7 %shard_map.55 = f32[1,400]{1,0:T(1,128)S(1)} custom-call(f32[1,400]{1,0:T(1,128)} %bitcast.3, bf16[4,10000]{1,0:T(4,128)(2,1)} %diag_hbm.1, bf16[4,40000]{1,0:T(4,128)(2,1)} %face_hbm.1, bf16[4,10000]{1,0:T(4,128)(2,1)} %prec_hbm.1, s32[4,4]{1,0:T(4,128)} %near_hbm.1), custom_call_target="tpu_custom_call" | custom-call | flops 2000000 | bytes 500000 | tf_op jit(solution)/shard_map/pallas_call | solution.py:364
  30.7 0.6 %copy.7 = f32[400]{0:T(512)} copy(f32[400]{0:T(512)S(1)} %bitcast.2) | data formatting | bytes 3200
